TPU v7x, 32 devices: a whole 2x2x4 slice. The times are simulated.
32 devices in a mesh: mem: 32 (over z, y, x, core).
Axes of the slice: x: 2, y: 2, z: 4, core: 2. Of those that a mesh axis runs over, the one named last changes fastest.
Arguments:
- query_feats: float32 [32768, 8], P('mem'), may hold values from -6 to 6
- feature_mask: int32 [32768, 8], P('mem'), may hold values from 0 to 1, as said below
- query_task: int32 [32768], P('mem'), may hold values from 0 to 3
- target_class: int32 [32768], P('mem'), may hold values from 0 to 15
- target_mask: int32 [32768], P('mem'), may hold values from 0 to 1, as said below
- memory_feats: float32 [2048, 8], P('mem'), may hold values from -6 to 6
- memory_task: int32 [2048], replicated, may hold values from 0 to 3, as said below
- memory_mask: int32 [2048], replicated, may hold values from 0 to 1, as said below
- anneal: float32 [1], replicated, may hold values from 0.3 to 0.7
- w_qkv: float32 [196608], P('mem'), may hold values from -0.375 to 0.375
- w_out: float32 [65536], P('mem'), may hold values from -6 to 6
- w_heads: float32 [6144], P('mem'), may hold values from -0.375 to 0.375
- w_small: float32 [1056], P('mem'), may hold values from 0.1 to 1.9
- m_qkv: float32 [196608], P('mem'), may hold values from -0.00015258789 to 0.00015258789
- m_out: float32 [65536], P('mem'), may hold values from -0.00015258789 to 0.00015258789
- m_heads: float32 [6144], P('mem'), may hold values from -0.00015258789 to 0.00015258789
- m_small: float32 [1056], P('mem'), may hold values from -0.00061035156 to 0.00061035156
- v_qkv: float32 [196608], P('mem'), may hold values from 9.536743e-12 to 3.814697e-11
- v_out: float32 [65536], P('mem'), may hold values from 9.536743e-13 to 3.8146973e-12
- v_heads: float32 [6144], P('mem'), may hold values from 9.536743e-12 to 3.814697e-11
- v_small: float32 [1056], P('mem'), may hold values from 1.5258789e-10 to 6.1035155e-10
Outputs:
- new_qkv: float32 [196608], P('mem')
- new_out: float32 [65536], P('mem')
- new_heads: float32 [6144], P('mem')
- new_small: float32 [1056], P('mem')
- first_qkv: float32 [196608], P('mem')
- first_out: float32 [65536], P('mem')
- first_heads: float32 [6144], P('mem')
- first_small: float32 [1056], P('mem')
- second_qkv: float32 [196608], P('mem')
- second_out: float32 [65536], P('mem')
- second_heads: float32 [6144], P('mem')
- second_small: float32 [1056], P('mem')
- copy_qkv: bfloat16 [196608], P('mem')
- copy_out: bfloat16 [65536], P('mem')
- copy_heads: bfloat16 [6144], P('mem')
- copy_small: bfloat16 [1056], P('mem')
- loss_value: float32 [1], replicated
- grad_norm: float32 [1], replicated
Inputs may be any that keep to these rules, and one draw needn't show every extreme that they name: `memory_mask`: the live rows of each device's 64 memory rows are a prefix of a quarter of them or more; the first device's rows are all live. `memory_task`: the first 4 memory rows have the tasks 0 to 3 in order. `target_mask`: the share of labelled queries rises along the query rows from about a quarter to about three quarters. `feature_mask`: the share of hidden features rises along the query rows from about a quarter to about three quarters.
All inputs are finite; a program needn't handle non-finite values.
Results may differ from a plain program's by a relative error of at most 0.0087.
Values may be sent and summed in bfloat16 or wider, within the bound.
A program may use at most 128 MiB of HBM per device.

v0:
```python
import math
import jax
import jax.numpy as jnp
from jax import lax
from jax.sharding import PartitionSpec as P

F = 8
D = 256
H = 8
C = 16
STEP = 10
eps_norm = 1e-05
max_norm = 0.05
beta_one = 0.9
beta_two = 0.999
adam_eps = 1e-08
decay_rate = 0.01
learn_rates = (0.05, 1.0, 0.05, 0.5)
masked_score = -1e30


def embed(feature_rows, table_flat, emb_bias):
    emb_table = table_flat.reshape(feature_rows.shape[1], -1)
    return (feature_rows[:, :, None] * emb_table[None]).reshape(
        feature_rows.shape[0], -1
    ) + emb_bias


def standard(hidden):
    centred = hidden - jnp.mean(hidden, -1, keepdims=True)
    inverse = lax.rsqrt(jnp.mean(centred * centred, -1, keepdims=True) + eps_norm)
    return (centred * inverse, inverse)


def norm_back(grad_out, hidden, gain_vec):
    normed, inverse = standard(hidden)
    grad_gain = jnp.sum(grad_out * normed, 0)
    grad_scaled = grad_out * gain_vec
    grad_hidden = inverse * (
        grad_scaled
        - jnp.mean(grad_scaled, -1, keepdims=True)
        - normed * jnp.mean(grad_scaled * normed, -1, keepdims=True)
    )
    return (grad_hidden, grad_gain)


def split_pair(values):
    upper = values.astype(jnp.bfloat16)
    lower = (values - upper.astype(jnp.float32)).astype(jnp.bfloat16)
    return (upper, lower)


def adamw(weight, first_mom, second, grad_in, factor, step_num, step_rate):
    clipped = grad_in * factor
    first_new = beta_one * first_mom + (1 - beta_one) * clipped
    second_new = beta_two * second + (1 - beta_two) * clipped * clipped
    fix_one = 1 - beta_one**step_num
    fix_two = 1 - beta_two**step_num
    weight_new = weight - step_rate * (
        first_new / fix_one / (jnp.sqrt(second_new / fix_two) + adam_eps) + decay_rate * weight
    )
    return (first_new, second_new, weight_new)


def local(
    query_feats,
    feature_mask,
    query_task,
    target_class,
    target_mask,
    memory_feats,
    memory_task,
    memory_mask,
    anneal,
    w_qkv,
    w_out,
    w_heads,
    w_small,
    m_qkv,
    m_out,
    m_heads,
    m_small,
    v_qkv,
    v_out,
    v_heads,
    v_small,
):
    high = lax.Precision.HIGHEST
    head_size = D // H
    full_qkv, full_out, full_heads, full_small = (
        lax.all_gather(w_qkv, "mem", axis=0, tiled=True),
        lax.all_gather(w_out, "mem", axis=0, tiled=True),
        lax.all_gather(w_heads, "mem", axis=0, tiled=True),
        lax.all_gather(w_small, "mem", axis=0, tiled=True),
    )
    emb_table = full_small[:D]
    emb_bias = full_small[D : 2 * D]
    gain_in = full_small[2 * D : 3 * D]
    gain_out = full_small[3 * D : 4 * D]
    score_coef = full_small[4 * D : 4 * D + H] * head_size ** (-0.5)
    qkv_low = full_qkv.reshape(D, 3 * D).astype(jnp.bfloat16)
    out_low = full_out.reshape(D, D).astype(jnp.bfloat16)
    heads_low = full_heads.reshape(D, C + F).astype(jnp.bfloat16)
    mem_hidden = embed(memory_feats, emb_table, emb_bias)
    mem_normed = (standard(mem_hidden)[0] * gain_in).astype(jnp.bfloat16)
    mem_kv = jnp.dot(mem_normed, qkv_low[:, D:], preferred_element_type=jnp.float32).astype(
        jnp.bfloat16
    )
    all_kv = lax.all_gather(mem_kv, "mem", axis=0, tiled=True)
    memory_rows = all_kv.shape[0]
    block_keys = math.gcd(memory_rows, 512)
    num_blocks = memory_rows // block_keys
    key_rows = all_kv[:, :D].reshape(num_blocks, block_keys, H, head_size)
    value_rows = all_kv[:, D:].reshape(num_blocks, block_keys, H, head_size)
    task_blocks = memory_task.reshape(num_blocks, block_keys)
    live_blocks = memory_mask.reshape(num_blocks, block_keys)
    key_blocks = (key_rows, value_rows, task_blocks, live_blocks)
    kept_input = query_feats * (1 - feature_mask).astype(jnp.float32)
    hidden_in = embed(kept_input, emb_table, emb_bias)
    query_normed = (standard(hidden_in)[0] * gain_in).astype(jnp.bfloat16)
    queries = (
        jnp.dot(query_normed, qkv_low[:, :D], preferred_element_type=jnp.float32)
        .astype(jnp.bfloat16)
        .reshape(-1, H, head_size)
    )
    num_rows = queries.shape[0]

    def allowed_of(task_row, live_row):
        return ((query_task[:, None] == task_row[None, :]) & (live_row[None, :] > 0))[None]

    def scores_of(key_block, allowed):
        raw_scores = jnp.einsum(
            "qhd,khd->hqk", queries, key_block, preferred_element_type=jnp.float32
        )
        return (
            raw_scores,
            jnp.where(allowed, score_coef[:, None, None] * raw_scores, masked_score),
        )

    def stats_step(state_in, block_data):
        row_top, row_sum = state_in
        key_block, value_block, task_row, live_row = block_data
        allowed = allowed_of(task_row, live_row)
        scores = scores_of(key_block, allowed)[1]
        new_top = jnp.maximum(row_top, jnp.max(scores, -1))
        shifted = jnp.where(allowed, jnp.exp(scores - new_top[..., None]), 0.0)
        return ((new_top, row_sum * jnp.exp(row_top - new_top) + jnp.sum(shifted, -1)), None)

    start_state = (
        jnp.full((H, num_rows), masked_score, jnp.float32),
        jnp.zeros((H, num_rows), jnp.float32),
    )
    (row_top, row_sum), unused = lax.scan(stats_step, start_state, key_blocks)

    def probs_of(scores, allowed):
        return jnp.where(allowed, jnp.exp(scores - row_top[..., None]), 0.0) / row_sum[..., None]

    def value_step(accum, block_data):
        key_block, value_block, task_row, live_row = block_data
        allowed = allowed_of(task_row, live_row)
        probs_low = probs_of(scores_of(key_block, allowed)[1], allowed).astype(jnp.bfloat16)
        return (
            accum
            + jnp.einsum(
                "hqk,khd->qhd", probs_low, value_block, preferred_element_type=jnp.float32
            ),
            None,
        )

    attn_sum, unused = lax.scan(
        value_step, jnp.zeros((num_rows, H, head_size), jnp.float32), key_blocks
    )
    attended = attn_sum.reshape(num_rows, D).astype(jnp.bfloat16)
    residual = hidden_in + jnp.dot(attended, out_low, preferred_element_type=jnp.float32)
    final_normed = (standard(residual)[0] * gain_out).astype(jnp.bfloat16)
    head_out = jnp.dot(final_normed, heads_low, preferred_element_type=jnp.float32)
    logits = head_out[:, :C]
    recon_err = head_out[:, C:] - query_feats
    label_mask = target_mask.astype(jnp.float32)
    feat_mask = feature_mask.astype(jnp.float32)
    onehot_class = jax.nn.one_hot(target_class, C, dtype=jnp.float32)
    picked = jnp.sum(logits * onehot_class, -1)
    sum_target, sum_recon, count_target, count_recon = lax.psum(
        (
            jnp.sum(label_mask * (jax.nn.logsumexp(logits, -1) - picked)),
            jnp.sum(feat_mask * recon_err**2),
            jnp.sum(label_mask),
            jnp.sum(feat_mask),
        ),
        "mem",
    )
    count_target = jnp.maximum(count_target, 1.0)
    count_recon = jnp.maximum(count_recon, 1.0)
    weight_a = anneal[0]
    loss_value = weight_a * sum_target / count_target + (1 - weight_a) * sum_recon / count_recon
    grad_logits = (
        weight_a / count_target * label_mask[:, None] * (jax.nn.softmax(logits, -1) - onehot_class)
    )
    grad_recon = (1 - weight_a) / count_recon * feat_mask * 2.0 * recon_err
    grad_head_out = jnp.concatenate([grad_logits, grad_recon], 1).astype(jnp.bfloat16)
    grad_heads = jnp.dot(final_normed.T, grad_head_out, preferred_element_type=jnp.float32)
    grad_final = jnp.dot(grad_head_out, heads_low.T, preferred_element_type=jnp.float32)
    grad_resid, grad_gain_out = norm_back(grad_final, residual, gain_out)
    grad_branch = grad_resid.astype(jnp.bfloat16)
    grad_wout = jnp.dot(attended.T, grad_branch, preferred_element_type=jnp.float32)
    grad_attn = (
        jnp.dot(grad_branch, out_low.T, preferred_element_type=jnp.float32)
        .astype(jnp.bfloat16)
        .reshape(num_rows, H, head_size)
    )
    row_delta = jnp.sum(
        grad_attn.astype(jnp.float32)
        * attended.reshape(num_rows, H, head_size).astype(jnp.float32),
        -1,
    ).T

    def back_step(state_in, block_data):
        key_block, value_block, task_row, live_row = block_data
        allowed = allowed_of(task_row, live_row)
        raw_scores, scores = scores_of(key_block, allowed)
        soft_probs = probs_of(scores, allowed)
        grad_probs = jnp.einsum(
            "qhd,khd->hqk", grad_attn, value_block, preferred_element_type=jnp.float32
        )
        grad_scores = (soft_probs * (grad_probs - row_delta[..., None])).astype(jnp.bfloat16)
        grad_beta = jnp.sum(grad_scores.astype(jnp.float32) * raw_scores, (1, 2))
        grad_query = jnp.einsum(
            "hqk,khd->qhd", grad_scores, key_block, preferred_element_type=jnp.float32
        )
        grad_key = (
            jnp.einsum("hqk,qhd->khd", grad_scores, queries, preferred_element_type=jnp.float32)
            * score_coef[None, :, None]
        )
        grad_value = jnp.einsum(
            "hqk,qhd->khd",
            soft_probs.astype(jnp.bfloat16),
            grad_attn,
            preferred_element_type=jnp.float32,
        )
        block_rows = key_block.shape[0]
        grad_kv = jnp.concatenate(
            [grad_key.reshape(block_rows, D), grad_value.reshape(block_rows, D)], 1
        )
        return ((state_in[0] + grad_query, state_in[1] + grad_beta), grad_kv)

    init_state = (jnp.zeros((num_rows, H, head_size), jnp.float32), jnp.zeros((H,), jnp.float32))
    (grad_q_sum, grad_beta_sum), kv_parts = lax.scan(back_step, init_state, key_blocks)
    kv_grad = lax.psum_scatter(
        kv_parts.reshape(memory_rows, 2 * D), "mem", scatter_dimension=0, tiled=True
    )
    grad_q_low = (grad_q_sum * score_coef[None, :, None]).reshape(num_rows, D).astype(jnp.bfloat16)
    grad_wq = jnp.dot(query_normed.T, grad_q_low, preferred_element_type=jnp.float32)
    grad_qn = jnp.dot(grad_q_low, qkv_low[:, :D].T, preferred_element_type=jnp.float32)
    grad_in_q, gain_in_q = norm_back(grad_qn, hidden_in, gain_in)
    grad_hidden = grad_resid + grad_in_q
    kv_upper, kv_lower = split_pair(kv_grad)
    grad_wkv = jnp.dot(mem_normed.T, kv_upper, preferred_element_type=jnp.float32) + jnp.dot(
        mem_normed.T, kv_lower, preferred_element_type=jnp.float32
    )
    grad_mn = jnp.dot(kv_upper, qkv_low[:, D:].T, preferred_element_type=jnp.float32) + jnp.dot(
        kv_lower, qkv_low[:, D:].T, preferred_element_type=jnp.float32
    )
    grad_mem, gain_in_m = norm_back(grad_mn, mem_hidden, gain_in)
    grad_table = jnp.einsum(
        "qf,qfe->fe", kept_input, grad_hidden.reshape(num_rows, F, -1), precision=high
    )
    grad_table = grad_table + jnp.einsum(
        "qf,qfe->fe", memory_feats, grad_mem.reshape(memory_feats.shape[0], F, -1), precision=high
    )
    grad_bias = jnp.sum(grad_hidden, 0) + jnp.sum(grad_mem, 0)
    small_size = full_small.shape[0]
    grad_small = jnp.concatenate(
        [
            grad_table.reshape(-1),
            grad_bias,
            gain_in_q + gain_in_m,
            grad_gain_out,
            grad_beta_sum * head_size ** (-0.5),
            jnp.zeros((small_size - 4 * D - H,), jnp.float32),
        ]
    )
    grad_qkv = jnp.concatenate([grad_wq, grad_wkv], 1).reshape(-1)
    shards = (
        lax.psum_scatter(grad_qkv, "mem", scatter_dimension=0, tiled=True),
        lax.psum_scatter(grad_wout.reshape(-1), "mem", scatter_dimension=0, tiled=True),
        lax.psum_scatter(grad_heads.reshape(-1), "mem", scatter_dimension=0, tiled=True),
        lax.psum_scatter(grad_small, "mem", scatter_dimension=0, tiled=True),
    )
    local_squares = sum((jnp.sum(piece_grad * piece_grad) for piece_grad in shards))
    grad_total = jnp.sqrt(lax.psum(local_squares, "mem"))
    factor = jnp.minimum(1.0, max_norm / (grad_total + 1e-06))
    step_num = float(STEP)
    weights_all = (w_qkv, w_out, w_heads, w_small)
    firsts = (m_qkv, m_out, m_heads, m_small)
    seconds = (v_qkv, v_out, v_heads, v_small)
    results = [
        adamw(weight, first_mom, second, grad_in, factor, step_num, step_rate)
        for weight, first_mom, second, grad_in, step_rate in zip(
            weights_all, firsts, seconds, shards, learn_rates
        )
    ]
    new_w = [entry[2] for entry in results]
    return (
        new_w[0],
        new_w[1],
        new_w[2],
        new_w[3],
        results[0][0],
        results[1][0],
        results[2][0],
        results[3][0],
        results[0][1],
        results[1][1],
        results[2][1],
        results[3][1],
        new_w[0].astype(jnp.bfloat16),
        new_w[1].astype(jnp.bfloat16),
        new_w[2].astype(jnp.bfloat16),
        new_w[3].astype(jnp.bfloat16),
        loss_value.reshape(1),
        grad_total.reshape(1),
    )


def solution(mesh):
    placed = (
        P("mem", None),
        P("mem", None),
        P("mem"),
        P("mem"),
        P("mem"),
        P("mem", None),
        P(),
        P(),
        P(),
        P("mem"),
        P("mem"),
        P("mem"),
        P("mem"),
        P("mem"),
        P("mem"),
        P("mem"),
        P("mem"),
        P("mem"),
        P("mem"),
        P("mem"),
        P("mem"),
    )
    return jax.shard_map(
        local,
        mesh=mesh,
        in_specs=placed,
        out_specs=(
            P("mem"),
            P("mem"),
            P("mem"),
            P("mem"),
            P("mem"),
            P("mem"),
            P("mem"),
            P("mem"),
            P("mem"),
            P("mem"),
            P("mem"),
            P("mem"),
            P("mem"),
            P("mem"),
            P("mem"),
            P("mem"),
            P(),
            P(),
        ),
        check_vma=False,
    )
```

profile of v0, /device:TPU:0, one launch (start us, length us, event | category | flops | bytes accessed | tf_op | source)
XLA Modules:
  0.0 763.1 jit_solution(16829456224447970304)
XLA Ops:
  9.7 42.3 %all-reduce.9 = (f32[1056]{0:T(1024)S(1)}, bf16[6144]{0:T(1024)(128)(2,1)S(1)}) all-reduce(f32[1056]{0:T(1024)S(1)} %dynamic-update-slice, f32[6144]{0:T(1024)S(1)} %dynamic-update-slice.1), channel_id=1, replica_groups=mesh['mem'=32] {'mem'}, use_global_device_ids=true, to_apply=%add | all-reduce | flops 7200 | bytes 45312
  55.3 41.3 %all_gather.16 = bf16[196608]{0:T(1024)(128)(2,1)S(1)} all-gather(bf16[6144]{0:T(1024)(128)(2,1)S(1)} %convert.24), channel_id=1, replica_groups=mesh['mem'=32] {'mem'}, dimensions={0}, use_global_device_ids=true | all-gather | bytes 405504 | tf_op jit(solution)/shard_map/all_gather | solution.py:91
  101.4 37.2 %all_gather.18 = bf16[65536]{0:T(1024)(128)(2,1)S(1)} all-gather(bf16[2048]{0:T(1024)(128)(2,1)S(1)} %convert.25), channel_id=1, replica_groups=mesh['mem'=32] {'mem'}, dimensions={0}, use_global_device_ids=true | all-gather | bytes 135168 | tf_op jit(solution)/shard_map/all_gather | solution.py:92
  142.2 8.4 %all-gather.2.cloned.1.call-done = bf16[2048,512]{1,0:T(8,128)(2,1)} async-done(((bf16[64,512]{1,0:T(8,128)(2,1)}), bf16[2048,512]{1,0:T(8,128)(2,1)}) %all-gather.2.cloned.1.call-update) | async-done | bytes 2097168 | tf_op jit(solution)/shard_map/all_gather | solution.py:109
  159.5 35.7 %while.39 = (s32[]{:T(128)}, f32[8,1024]{1,0:T(8,128)S(1)}, f32[8,1024]{1,0:T(8,128)S(1)}, s32[1024]{0:T(1024)S(1)}, s32[4,512]{1,0:T(4,128)S(1)}, /*index=5*/s3...) while((s32[]{:T(128)}, f32[8,1024]{1,0:T(8,128)S(1)}, ...), condition=%wide.region_7.8_spmd.clone, body=%wide.region_4.7_spmd.clone.sunk | while | flops 303079936 | bytes 36353224 | solution.py:153
  164.1 4.3 select_reduce_fusion.3
  173.0 4.3 select_reduce_fusion.3
  182.0 4.3 select_reduce_fusion.3
  190.9 4.3 select_reduce_fusion.3
  195.3 33.3 %while.40 = (s32[]{:T(128)}, f32[1024,8,32]{0,2,1:T(8,128)S(1)}, bf16[4,512,8,32]{1,3,2,0:T(8,128)(2,1)}, s32[1024]{0:T(1024)S(1)}, s32[4,512]{1,0:T(4,128)S(1)}...) while((s32[]{:T(128)}, f32[1024,8,32]{0,2,1:T(8,128)S(1)}, ...), condition=%wide.region_9.10_spmd.clone, body=%wide.region_8.9_spmd.clone.sunk | while | flops 563610112 | bytes 4274870 | solution.py:170
  196.3 7.7 %fusion.145 = f32[1024,8,32]{0,2,1:T(8,128)S(1)} fusion(bf16[1024,8,32]{0,2,1:T(8,128)(2,1)S(1)} %get-tuple-element.853, f32[8,1024]{1,0:T(8,128)S(1)} %get-tuple-element.855, f32[8,1024]{1,0:T(8,128)S(1)} %get-tuple-element.854, f32[8]{0:T(128)S(1)} %get-tuple-element.851, pred[1024,512]{0,1:T(8,128)(4,1)S(1)} %compare_and_fusion.7, ...), kind=kOutput, calls=%fused_computation.28.clone.1 | convolution fusion | flops 562561024 | bytes 3737120 | tf_op jit(solution)/shard_map/while/body/eval_jaxpr/hqk,khd->qhd/dot_general | solution.py:164
  204.5 7.7 %fusion.145 = f32[1024,8,32]{0,2,1:T(8,128)S(1)} fusion(bf16[1024,8,32]{0,2,1:T(8,128)(2,1)S(1)} %get-tuple-element.853, f32[8,1024]{1,0:T(8,128)S(1)} %get-tuple-element.855, f32[8,1024]{1,0:T(8,128)S(1)} %get-tuple-element.854, f32[8]{0:T(128)S(1)} %get-tuple-element.851, pred[1024,512]{0,1:T(8,128)(4,1)S(1)} %compare_and_fusion.7, ...), kind=kOutput, calls=%fused_computation.28.clone.1 | convolution fusion | flops 562561024 | bytes 3737120 | tf_op jit(solution)/shard_map/while/body/eval_jaxpr/hqk,khd->qhd/dot_general | solution.py:164
  212.7 7.7 %fusion.145 = f32[1024,8,32]{0,2,1:T(8,128)S(1)} fusion(bf16[1024,8,32]{0,2,1:T(8,128)(2,1)S(1)} %get-tuple-element.853, f32[8,1024]{1,0:T(8,128)S(1)} %get-tuple-element.855, f32[8,1024]{1,0:T(8,128)S(1)} %get-tuple-element.854, f32[8]{0:T(128)S(1)} %get-tuple-element.851, pred[1024,512]{0,1:T(8,128)(4,1)S(1)} %compare_and_fusion.7, ...), kind=kOutput, calls=%fused_computation.28.clone.1 | convolution fusion | flops 562561024 | bytes 3737120 | tf_op jit(solution)/shard_map/while/body/eval_jaxpr/hqk,khd->qhd/dot_general | solution.py:164
  220.9 7.7 %fusion.145 = f32[1024,8,32]{0,2,1:T(8,128)S(1)} fusion(bf16[1024,8,32]{0,2,1:T(8,128)(2,1)S(1)} %get-tuple-element.853, f32[8,1024]{1,0:T(8,128)S(1)} %get-tuple-element.855, f32[8,1024]{1,0:T(8,128)S(1)} %get-tuple-element.854, f32[8]{0:T(128)S(1)} %get-tuple-element.851, pred[1024,512]{0,1:T(8,128)(4,1)S(1)} %compare_and_fusion.7, ...), kind=kOutput, calls=%fused_computation.28.clone.1 | convolution fusion | flops 562561024 | bytes 3737120 | tf_op jit(solution)/shard_map/while/body/eval_jaxpr/hqk,khd->qhd/dot_general | solution.py:164
  234.2 38.8 %all-reduce.8 = (f32[]{:T(128)}, f32[]{:T(128)}) all-reduce(f32[]{:T(128)} %get-tuple-element.440, f32[]{:T(128)} %get-tuple-element.442), channel_id=1, replica_groups=mesh['mem'=32] {'mem'}, use_global_device_ids=true, to_apply=%region_17.18 | all-reduce | flops 2 | bytes 16 | tf_op jit(solution)/shard_map/psum | solution.py:183
  278.5 150.5 %while.41 = (s32[]{:T(128)}, f32[1024,8,32]{0,2,1:T(8,128)}, f32[8]{0:T(128)}, f32[4,512,512]{2,1,0:T(8,128)}, bf16[4,512,8,32]{1,3,2,0:T(8,128)(2,1)}, /*index=...) while((s32[]{:T(128)}, f32[1024,8,32]{0,2,1:T(8,128)}, ...), condition=%wide.region_23.24_spmd.clone, body=%wide.region_21.23_spmd.clone.sunk | while | flops 1415447040 | bytes 156940240 | solution.py:247
  283.3 5.7 copy-done
  289.0 6.7 fusion.159
  295.7 12.7 %fusion.156 = (f32[8]{0:T(128)S(1)}, bf16[8,1024,512]{1,2,0:T(8,128)(2,1)S(1)}) fusion(f32[8,512,1024]{2,1,0:T(8,128)} %copy-done, f32[8,1024]{1,0:T(8,128)} %get-tuple-element.906, bf16[1024,8,32]{0,2,1:T(8,128)(2,1)} %get-tuple-element.905, bf16[4,512,8,32]{1,3,2,0:T(8,128)(2,1)} %get-tuple-element.904, s32[]{:T(128)S(6)} %copy.149, ...), kind=kOutput, calls=%fused_computation.47.clone.1 | convolution fusion | flops 314572800 | bytes 26574916 | tf_op jit(solution)/shard_map/while/body/eval_jaxpr/qhd,khd->hqk/dot_general | solution.py:222
  320.5 5.7 copy-done
  326.2 6.7 fusion.159
  332.9 12.7 %fusion.156 = (f32[8]{0:T(128)S(1)}, bf16[8,1024,512]{1,2,0:T(8,128)(2,1)S(1)}) fusion(f32[8,512,1024]{2,1,0:T(8,128)} %copy-done, f32[8,1024]{1,0:T(8,128)} %get-tuple-element.906, bf16[1024,8,32]{0,2,1:T(8,128)(2,1)} %get-tuple-element.905, bf16[4,512,8,32]{1,3,2,0:T(8,128)(2,1)} %get-tuple-element.904, s32[]{:T(128)S(6)} %copy.149, ...), kind=kOutput, calls=%fused_computation.47.clone.1 | convolution fusion | flops 314572800 | bytes 26574916 | tf_op jit(solution)/shard_map/while/body/eval_jaxpr/qhd,khd->hqk/dot_general | solution.py:222
  358.1 5.7 copy-done
  363.9 6.7 fusion.159
  370.5 12.7 %fusion.156 = (f32[8]{0:T(128)S(1)}, bf16[8,1024,512]{1,2,0:T(8,128)(2,1)S(1)}) fusion(f32[8,512,1024]{2,1,0:T(8,128)} %copy-done, f32[8,1024]{1,0:T(8,128)} %get-tuple-element.906, bf16[1024,8,32]{0,2,1:T(8,128)(2,1)} %get-tuple-element.905, bf16[4,512,8,32]{1,3,2,0:T(8,128)(2,1)} %get-tuple-element.904, s32[]{:T(128)S(6)} %copy.149, ...), kind=kOutput, calls=%fused_computation.47.clone.1 | convolution fusion | flops 314572800 | bytes 26574916 | tf_op jit(solution)/shard_map/while/body/eval_jaxpr/qhd,khd->hqk/dot_general | solution.py:222
  395.7 5.7 copy-done
  401.4 6.7 fusion.159
  408.1 12.7 %fusion.156 = (f32[8]{0:T(128)S(1)}, bf16[8,1024,512]{1,2,0:T(8,128)(2,1)S(1)}) fusion(f32[8,512,1024]{2,1,0:T(8,128)} %copy-done, f32[8,1024]{1,0:T(8,128)} %get-tuple-element.906, bf16[1024,8,32]{0,2,1:T(8,128)(2,1)} %get-tuple-element.905, bf16[4,512,8,32]{1,3,2,0:T(8,128)(2,1)} %get-tuple-element.904, s32[]{:T(128)S(6)} %copy.149, ...), kind=kOutput, calls=%fused_computation.47.clone.1 | convolution fusion | flops 314572800 | bytes 26574916 | tf_op jit(solution)/shard_map/while/body/eval_jaxpr/qhd,khd->hqk/dot_general | solution.py:222
  442.5 128.2 %reduce-scatter.2.cloned.1.call-done = f32[64,512]{1,0:T(8,128)} async-done(((f32[2048,512]{1,0:T(8,128)}), f32[64,512]{1,0:T(8,128)}) %reduce-scatter.2.cloned.1.call-update) | async-done | bytes 131088 | tf_op jit(solution)/shard_map/reduce_scatter | solution.py:248
  577.5 37.4 %all-reduce.7 = (f32[6144]{0:T(1024)S(1)}, f32[1056]{0:T(1024)S(1)}) all-reduce(f32[6144]{0:T(1024)S(1)} %reshape.518, f32[1056]{0:T(1024)S(1)} %concatenate.15), channel_id=5, replica_groups=mesh['mem'=32] {'mem'}, use_global_device_ids=true, to_apply=%region_29.30.clone | all-reduce | flops 7200 | bytes 57600
  616.3 86.9 %all-reduce.13.cloned.1.call-done = (f32[196608]{0:T(1024)}, f32[65536]{0:T(1024)}) async-done(((f32[196608]{0:T(1024)}, f32[65536]{0:T(1024)}), (f32[196608]{0:T(1024)}, f32[65536]{0:T(1024)})) %all-reduce.13.cloned.1.call-update) | async-done | bytes 1048592
  708.4 39.5 %all-reduce.6 = (f32[]{:T(128)}, f32[]{:T(128)}, f32[]{:T(128)}) all-reduce(f32[]{:T(128)S(6)} %add.225, f32[]{:T(128)} %get-tuple-element.441, f32[]{:T(128)} %get-tuple-element.439), channel_id=1, replica_groups=mesh['mem'=32] {'mem'}, use_global_device_ids=true, to_apply=%region_42.43 | all-reduce | flops 3 | bytes 24 | tf_op jit(solution)/shard_map/psum | solution.py:290
  (340 shorter events, 129.4 us)
Async XLA Ops:
  7.2 152.2 %copy-start.16 = (s32[1024]{0:T(1024)S(1)}, s32[1024]{0:T(1024)}, u32[]{:S(2)}) copy-start(s32[1024]{0:T(1024)} %param.29) | copy-start | bytes 12292
  7.2 143.3 %all-gather.2.cloned.1.call-start = ((), (), s32[]{:S(2)}) async-start(), calls=%async_computation.1 | async-start | bytes 2162688 | tf_op jit(solution)/shard_map/all_gather | solution.py:109
  52.6 106.8 %copy-start.33 = (f32[256]{0:T(256)}, f32[256]{0:T(256)S(1)}, u32[]{:S(2)}) copy-start(f32[256]{0:T(256)S(1)} %get-tuple-element.553) | copy-start | bytes 3076
  52.6 106.8 %copy-start.35 = (f32[256]{0:T(256)}, f32[256]{0:T(256)S(1)}, u32[]{:S(2)}) copy-start(f32[256]{0:T(256)S(1)} %get-tuple-element.554) | copy-start | bytes 3076
  52.6 106.8 %copy-start.37 = (f32[256]{0:T(256)}, f32[256]{0:T(256)S(1)}, u32[]{:S(2)}) copy-start(f32[256]{0:T(256)S(1)} %get-tuple-element.555) | copy-start | bytes 3076
  52.7 106.8 %copy-start.27 = (f32[8,32]{1,0:T(8,128)}, f32[8,32]{1,0:T(8,128)S(1)}, u32[]{:S(2)}) copy-start(f32[8,32]{1,0:T(8,128)S(1)} %add.204) | copy-start | bytes 3076
  52.8 106.7 %copy-start.28 = (f32[8,32]{1,0:T(8,128)}, f32[8,32]{1,0:T(8,128)S(1)}, u32[]{:S(2)}) copy-start(f32[8,32]{1,0:T(8,128)S(1)} %mul.534) | copy-start | bytes 3076
  97.8 472.9 %reduce-scatter.2.cloned.1.call-start = ((), (), s32[]{:S(2)}) async-start(), calls=%async_computation.2 | async-start | bytes 4325376 | tf_op jit(solution)/shard_map/reduce_scatter | solution.py:248
  278.5 151.6 %copy-start.25 = (f32[1024]{0:T(1024)S(1)}, f32[1024]{0:T(1024)}, u32[]{:S(2)}) copy-start(f32[1024]{0:T(1024)} %copy-done.24) | copy-start | bytes 12292
  278.5 152.7 %copy-start.4 = (bf16[1024,256]{0,1:T(8,128)(2,1)S(1)}, bf16[1024,256]{0,1:T(8,128)(2,1)}, u32[]{:S(2)}) copy-start(bf16[1024,256]{0,1:T(8,128)(2,1)} %copy-done.3) | copy-start | bytes 1572868
  278.5 157.9 %copy-start.7 = (bf16[256,768]{1,0:T(8,128)(2,1)S(1)}, bf16[256,768]{1,0:T(8,128)(2,1)}, u32[]{:S(2)}) copy-start(bf16[256,768]{1,0:T(8,128)(2,1)} %copy-done.6) | copy-start | bytes 1179652
  429.0 142.8 %copy-start.12 = (f32[64,256]{1,0:T(8,128)S(1)}, f32[64,256]{1,0:T(8,128)}, u32[]{:S(2)}) copy-start(f32[64,256]{1,0:T(8,128)} %copy-done.11) | copy-start | bytes 196612
  429.0 142.8 %copy-start.34 = (f32[256]{0:T(256)S(1)}, f32[256]{0:T(256)}, u32[]{:S(2)}) copy-start(f32[256]{0:T(256)} %copy-done.33) | copy-start | bytes 3076
  429.0 142.8 %copy-start.36 = (f32[256]{0:T(256)S(1)}, f32[256]{0:T(256)}, u32[]{:S(2)}) copy-start(f32[256]{0:T(256)} %copy-done.35) | copy-start | bytes 3076
  429.0 142.8 %copy-start.38 = (f32[256]{0:T(256)S(1)}, f32[256]{0:T(256)}, u32[]{:S(2)}) copy-start(f32[256]{0:T(256)} %copy-done.37) | copy-start | bytes 3076
  429.0 142.8 %copy-start.47 = (f32[64]{0:T(128)S(1)}, f32[64]{0:T(128)}, u32[]{:S(2)}) copy-start(f32[64]{0:T(128)} %copy-done.46) | copy-start | bytes 772
  429.1 142.8 %copy-start.51 = (f32[64]{0:T(128)S(1)}, f32[64]{0:T(128)}, u32[]{:S(2)}) copy-start(f32[64]{0:T(128)} %copy-done.50) | copy-start | bytes 772
  429.1 147.9 %copy-start.39 = (f32[64,8]{0,1:T(8,128)S(1)}, f32[64,8]{0,1:T(8,128)}, u32[]{:S(2)}) copy-start(f32[64,8]{0,1:T(8,128)} %param.32) | copy-start | bytes 6148
  429.1 148.4 %copy-start.54 = (f32[256]{0:T(256)S(1)}, f32[256]{0:T(256)}, u32[]{:S(2)}) copy-start(f32[256]{0:T(256)} %get-tuple-element.427) | copy-start | bytes 3076
  429.1 321.0 %copy-start.32 = (f32[6144]{0:T(1024)S(1)}, f32[6144]{0:T(1024)}, u32[]{:S(2)}) copy-start(f32[6144]{0:T(1024)} %param.36) | copy-start | bytes 73732
  429.1 321.0 %copy-start.41 = (f32[6144]{0:T(1024)S(1)}, f32[6144]{0:T(1024)}, u32[]{:S(2)}) copy-start(f32[6144]{0:T(1024)} %param.40) | copy-start | bytes 73732
  429.1 321.0 %copy-start.42 = (f32[6144]{0:T(1024)S(1)}, f32[6144]{0:T(1024)}, u32[]{:S(2)}) copy-start(f32[6144]{0:T(1024)} %param.44) | copy-start | bytes 73732
  429.1 322.3 %copy-start.40 = (f32[2048]{0:T(1024)S(1)}, f32[2048]{0:T(1024)}, u32[]{:S(2)}) copy-start(f32[2048]{0:T(1024)} %param.37) | copy-start | bytes 24580
  429.1 322.3 %copy-start.52 = (f32[2048]{0:T(1024)S(1)}, f32[2048]{0:T(1024)}, u32[]{:S(2)}) copy-start(f32[2048]{0:T(1024)} %param.41) | copy-start | bytes 24580
  429.2 322.3 %copy-start.53 = (f32[2048]{0:T(1024)S(1)}, f32[2048]{0:T(1024)}, u32[]{:S(2)}) copy-start(f32[2048]{0:T(1024)} %param.45) | copy-start | bytes 24580
  429.2 323.6 %copy-start.55 = (f32[192]{0:T(256)S(1)}, f32[192]{0:T(256)}, u32[]{:S(2)}) copy-start(f32[192]{0:T(256)} %param.38) | copy-start | bytes 2308
  429.2 323.6 %copy-start.56 = (f32[192]{0:T(256)S(1)}, f32[192]{0:T(256)}, u32[]{:S(2)}) copy-start(f32[192]{0:T(256)} %param.42) | copy-start | bytes 2308
  429.2 323.6 %copy-start.57 = (f32[192]{0:T(256)S(1)}, f32[192]{0:T(256)}, u32[]{:S(2)}) copy-start(f32[192]{0:T(256)} %param.46) | copy-start | bytes 2308
  429.2 324.3 %copy-start.58 = (f32[33]{0:T(128)S(1)}, f32[33]{0:T(128)}, u32[]{:S(2)}) copy-start(f32[33]{0:T(128)} %param.39) | copy-start | bytes 400
  429.2 324.3 %copy-start.59 = (f32[33]{0:T(128)S(1)}, f32[33]{0:T(128)}, u32[]{:S(2)}) copy-start(f32[33]{0:T(128)} %param.43) | copy-start | bytes 400
  429.2 324.3 %copy-start.60 = (f32[33]{0:T(128)S(1)}, f32[33]{0:T(128)}, u32[]{:S(2)}) copy-start(f32[33]{0:T(128)} %param.47) | copy-start | bytes 400
  429.3 273.9 %all-reduce.13.cloned.1.call-start = ((), (), s32[]{:S(2)}) async-start(), calls=%async_computation.3 | async-start | bytes 2097152
  (50 other events, 1171.2 us)
Sparse Core Ops, SparseCore 0:
  97.9 52.5 all-gather.1
  429.4 141.2 reduce-scatter.1
  576.9 126.2 all-reduce.12
where the time goes:
time: 773 us; the launch traced here: 763 us
  blocking collectives  236 us (31%)
  waiting for transfers between devices  224 us (29%)
  matrix products  180 us (23%)
  local copies, waits for them, and re-layouts  49.9 us (6%)
  other arithmetic  47.9 us (6%)
  between operations  24 us (3%)
    reduce_scatter x1, waiting for transfers between devices, local(): lax.psum_scatter(kv_parts.reshape(memory_rows, 2 * D), 'mem', scatter_dim...  128 us
    unnamed x4, waiting for transfers between devices  86.9 us
    unnamed x2, blocking collectives  79.7 us
    dot_general x4, matrix products, back_step(): jnp.einsum('qhd,khd->hqk', grad_attn, value_block, preferred_element_type...  50.8 us
    all_gather x1, blocking collectives, local(): lax.all_gather(w_qkv, 'mem', axis=0, tiled=True)  41.3 us
    psum x1, blocking collectives, local(): grad_total = jnp.sqrt(lax.psum(local_squares, 'mem'))  39.5 us
    psum x1, blocking collectives, local(): lax.psum((jnp.sum(label_mask * (jax.nn.logsumexp(logits, -1) - picked)),...  38.8 us
    all_gather x1, blocking collectives, local(): lax.all_gather(w_out, 'mem', axis=0, tiled=True)  37.2 us
  transfers between devices with their start and end apart: 3, of which 3 were waited for; matrix products, arithmetic and copies ran while one was open for 3% of the time, Pallas kernels for 0%

commit v1 on v0

--- a/solution.py
+++ b/solution.py
@@ -17,6 +17,10 @@
 decay_rate = 0.01
 learn_rates = (0.05, 1.0, 0.05, 0.5)
 masked_score = -1e30
+
+
+def enter_members_all(mine_x):
+    return lax.all_gather(mine_x, "mem").sum(axis=0)
 
 
 def embed(feature_rows, table_flat, emb_bias):
@@ -287,7 +291,7 @@
         lax.psum_scatter(grad_small, "mem", scatter_dimension=0, tiled=True),
     )
     local_squares = sum((jnp.sum(piece_grad * piece_grad) for piece_grad in shards))
-    grad_total = jnp.sqrt(lax.psum(local_squares, "mem"))
+    grad_total = jnp.sqrt(enter_members_all(local_squares))
     factor = jnp.minimum(1.0, max_norm / (grad_total + 1e-06))
     step_num = float(STEP)
     weights_all = (w_qkv, w_out, w_heads, w_small)

time: 773 us -> 774 us (level)
    psum x1 -> x0, blocking collectives: 39.5 us -> none  [local(): grad_total = jnp.sqrt(lax.psum(local_squares, 'mem'))]
    unnamed x2 -> x3, blocking collectives: 79.7 us -> 119 us
where the time goes in v1:
time: 774 us; the launch traced here: 764 us
  blocking collectives  236 us (30%)
  waiting for transfers between devices  224 us (29%)
  matrix products  180 us (23%)
  local copies, waits for them, and re-layouts  50 us (6%)
  other arithmetic  48.5 us (6%)
  between operations  24 us (3%)
    reduce_scatter x1, waiting for transfers between devices, local(): lax.psum_scatter(kv_parts.reshape(memory_rows, 2 * D), 'mem', scatter_dim...  128 us
    unnamed x3, blocking collectives  119 us
    unnamed x4, waiting for transfers between devices  86.9 us
    dot_general x4, matrix products, back_step(): jnp.einsum('qhd,khd->hqk', grad_attn, value_block, preferred_element_type...  50.8 us
    all_gather x1, blocking collectives, local(): lax.all_gather(w_qkv, 'mem', axis=0, tiled=True)  41.3 us
    psum x1, blocking collectives, local(): lax.psum((jnp.sum(label_mask * (jax.nn.logsumexp(logits, -1) - picked)),...  38.8 us
    all_gather x1, blocking collectives, local(): lax.all_gather(w_out, 'mem', axis=0, tiled=True)  37.2 us
    dot_general x4, matrix products, value_step(): jnp.einsum('hqk,khd->qhd', probs_low, value_block, preferred_element_type...  30.9 us
  transfers between devices with their start and end apart: 3, of which 3 were waited for; matrix products, arithmetic and copies ran while one was open for 3% of the time, Pallas kernels for 0%

profile of v1, /device:TPU:0, one launch (start us, length us, event | category | flops | bytes accessed | tf_op | source)
XLA Modules:
  0.0 763.8 jit_solution(8605791139226970495)
XLA Ops:
  9.7 42.3 %all-reduce.10 = (f32[1056]{0:T(1024)S(1)}, bf16[6144]{0:T(1024)(128)(2,1)S(1)}) all-reduce(f32[1056]{0:T(1024)S(1)} %dynamic-update-slice, f32[6144]{0:T(1024)S(1)} %dynamic-update-slice.1), channel_id=1, replica_groups=mesh['mem'=32] {'mem'}, use_global_device_ids=true, to_apply=%add | all-reduce | flops 7200 | bytes 45312
  55.3 41.3 %all_gather.22 = bf16[196608]{0:T(1024)(128)(2,1)S(1)} all-gather(bf16[6144]{0:T(1024)(128)(2,1)S(1)} %convert.24), channel_id=1, replica_groups=mesh['mem'=32] {'mem'}, dimensions={0}, use_global_device_ids=true | all-gather | bytes 405504 | tf_op jit(solution)/shard_map/all_gather | solution.py:95
  101.4 37.2 %all_gather.24 = bf16[65536]{0:T(1024)(128)(2,1)S(1)} all-gather(bf16[2048]{0:T(1024)(128)(2,1)S(1)} %convert.25), channel_id=1, replica_groups=mesh['mem'=32] {'mem'}, dimensions={0}, use_global_device_ids=true | all-gather | bytes 135168 | tf_op jit(solution)/shard_map/all_gather | solution.py:96
  142.2 8.4 %all-gather.2.cloned.1.call-done = bf16[2048,512]{1,0:T(8,128)(2,1)} async-done(((bf16[64,512]{1,0:T(8,128)(2,1)}), bf16[2048,512]{1,0:T(8,128)(2,1)}) %all-gather.2.cloned.1.call-update) | async-done | bytes 2097168 | tf_op jit(solution)/shard_map/all_gather | solution.py:113
  159.5 35.7 %while.39 = (s32[]{:T(128)}, f32[8,1024]{1,0:T(8,128)S(1)}, f32[8,1024]{1,0:T(8,128)S(1)}, s32[1024]{0:T(1024)S(1)}, s32[4,512]{1,0:T(4,128)S(1)}, /*index=5*/s3...) while((s32[]{:T(128)}, f32[8,1024]{1,0:T(8,128)S(1)}, ...), condition=%wide.region_7.8_spmd.clone, body=%wide.region_4.7_spmd.clone.sunk | while | flops 303079936 | bytes 36353224 | solution.py:157
  164.1 4.3 select_reduce_fusion.3
  173.0 4.3 select_reduce_fusion.3
  182.0 4.3 select_reduce_fusion.3
  190.9 4.3 select_reduce_fusion.3
  195.3 33.3 %while.40 = (s32[]{:T(128)}, f32[1024,8,32]{0,2,1:T(8,128)S(1)}, bf16[4,512,8,32]{1,3,2,0:T(8,128)(2,1)}, s32[1024]{0:T(1024)S(1)}, s32[4,512]{1,0:T(4,128)S(1)}...) while((s32[]{:T(128)}, f32[1024,8,32]{0,2,1:T(8,128)S(1)}, ...), condition=%wide.region_9.10_spmd.clone, body=%wide.region_8.9_spmd.clone.sunk | while | flops 563610112 | bytes 4274870 | solution.py:174
  196.3 7.7 %fusion.145 = f32[1024,8,32]{0,2,1:T(8,128)S(1)} fusion(bf16[1024,8,32]{0,2,1:T(8,128)(2,1)S(1)} %get-tuple-element.853, f32[8,1024]{1,0:T(8,128)S(1)} %get-tuple-element.855, f32[8,1024]{1,0:T(8,128)S(1)} %get-tuple-element.854, f32[8]{0:T(128)S(1)} %get-tuple-element.851, pred[1024,512]{0,1:T(8,128)(4,1)S(1)} %compare_and_fusion.7, ...), kind=kOutput, calls=%fused_computation.28.clone.1 | convolution fusion | flops 562561024 | bytes 3737120 | tf_op jit(solution)/shard_map/while/body/eval_jaxpr/hqk,khd->qhd/dot_general | solution.py:168
  204.5 7.7 %fusion.145 = f32[1024,8,32]{0,2,1:T(8,128)S(1)} fusion(bf16[1024,8,32]{0,2,1:T(8,128)(2,1)S(1)} %get-tuple-element.853, f32[8,1024]{1,0:T(8,128)S(1)} %get-tuple-element.855, f32[8,1024]{1,0:T(8,128)S(1)} %get-tuple-element.854, f32[8]{0:T(128)S(1)} %get-tuple-element.851, pred[1024,512]{0,1:T(8,128)(4,1)S(1)} %compare_and_fusion.7, ...), kind=kOutput, calls=%fused_computation.28.clone.1 | convolution fusion | flops 562561024 | bytes 3737120 | tf_op jit(solution)/shard_map/while/body/eval_jaxpr/hqk,khd->qhd/dot_general | solution.py:168
  212.7 7.7 %fusion.145 = f32[1024,8,32]{0,2,1:T(8,128)S(1)} fusion(bf16[1024,8,32]{0,2,1:T(8,128)(2,1)S(1)} %get-tuple-element.853, f32[8,1024]{1,0:T(8,128)S(1)} %get-tuple-element.855, f32[8,1024]{1,0:T(8,128)S(1)} %get-tuple-element.854, f32[8]{0:T(128)S(1)} %get-tuple-element.851, pred[1024,512]{0,1:T(8,128)(4,1)S(1)} %compare_and_fusion.7, ...), kind=kOutput, calls=%fused_computation.28.clone.1 | convolution fusion | flops 562561024 | bytes 3737120 | tf_op jit(solution)/shard_map/while/body/eval_jaxpr/hqk,khd->qhd/dot_general | solution.py:168
  220.9 7.7 %fusion.145 = f32[1024,8,32]{0,2,1:T(8,128)S(1)} fusion(bf16[1024,8,32]{0,2,1:T(8,128)(2,1)S(1)} %get-tuple-element.853, f32[8,1024]{1,0:T(8,128)S(1)} %get-tuple-element.855, f32[8,1024]{1,0:T(8,128)S(1)} %get-tuple-element.854, f32[8]{0:T(128)S(1)} %get-tuple-element.851, pred[1024,512]{0,1:T(8,128)(4,1)S(1)} %compare_and_fusion.7, ...), kind=kOutput, calls=%fused_computation.28.clone.1 | convolution fusion | flops 562561024 | bytes 3737120 | tf_op jit(solution)/shard_map/while/body/eval_jaxpr/hqk,khd->qhd/dot_general | solution.py:168
  234.2 38.8 %all-reduce.9 = (f32[]{:T(128)}, f32[]{:T(128)}) all-reduce(f32[]{:T(128)} %get-tuple-element.440, f32[]{:T(128)} %get-tuple-element.442), channel_id=1, replica_groups=mesh['mem'=32] {'mem'}, use_global_device_ids=true, to_apply=%region_17.18 | all-reduce | flops 2 | bytes 16 | tf_op jit(solution)/shard_map/psum | solution.py:187
  278.5 150.5 %while.41 = (s32[]{:T(128)}, f32[1024,8,32]{0,2,1:T(8,128)}, f32[8]{0:T(128)}, f32[4,512,512]{2,1,0:T(8,128)}, bf16[4,512,8,32]{1,3,2,0:T(8,128)(2,1)}, /*index=...) while((s32[]{:T(128)}, f32[1024,8,32]{0,2,1:T(8,128)}, ...), condition=%wide.region_23.24_spmd.clone, body=%wide.region_21.23_spmd.clone.sunk | while | flops 1415447040 | bytes 156940240 | solution.py:251
  283.3 5.7 copy-done
  289.0 6.7 fusion.159
  295.7 12.7 %fusion.156 = (f32[8]{0:T(128)S(1)}, bf16[8,1024,512]{1,2,0:T(8,128)(2,1)S(1)}) fusion(f32[8,512,1024]{2,1,0:T(8,128)} %copy-done, f32[8,1024]{1,0:T(8,128)} %get-tuple-element.906, bf16[1024,8,32]{0,2,1:T(8,128)(2,1)} %get-tuple-element.905, bf16[4,512,8,32]{1,3,2,0:T(8,128)(2,1)} %get-tuple-element.904, s32[]{:T(128)S(6)} %copy.150, ...), kind=kOutput, calls=%fused_computation.47.clone.1 | convolution fusion | flops 314572800 | bytes 26574916 | tf_op jit(solution)/shard_map/while/body/eval_jaxpr/qhd,khd->hqk/dot_general | solution.py:226
  320.5 5.7 copy-done
  326.2 6.7 fusion.159
  332.9 12.7 %fusion.156 = (f32[8]{0:T(128)S(1)}, bf16[8,1024,512]{1,2,0:T(8,128)(2,1)S(1)}) fusion(f32[8,512,1024]{2,1,0:T(8,128)} %copy-done, f32[8,1024]{1,0:T(8,128)} %get-tuple-element.906, bf16[1024,8,32]{0,2,1:T(8,128)(2,1)} %get-tuple-element.905, bf16[4,512,8,32]{1,3,2,0:T(8,128)(2,1)} %get-tuple-element.904, s32[]{:T(128)S(6)} %copy.150, ...), kind=kOutput, calls=%fused_computation.47.clone.1 | convolution fusion | flops 314572800 | bytes 26574916 | tf_op jit(solution)/shard_map/while/body/eval_jaxpr/qhd,khd->hqk/dot_general | solution.py:226
  358.1 5.7 copy-done
  363.9 6.7 fusion.159
  370.5 12.7 %fusion.156 = (f32[8]{0:T(128)S(1)}, bf16[8,1024,512]{1,2,0:T(8,128)(2,1)S(1)}) fusion(f32[8,512,1024]{2,1,0:T(8,128)} %copy-done, f32[8,1024]{1,0:T(8,128)} %get-tuple-element.906, bf16[1024,8,32]{0,2,1:T(8,128)(2,1)} %get-tuple-element.905, bf16[4,512,8,32]{1,3,2,0:T(8,128)(2,1)} %get-tuple-element.904, s32[]{:T(128)S(6)} %copy.150, ...), kind=kOutput, calls=%fused_computation.47.clone.1 | convolution fusion | flops 314572800 | bytes 26574916 | tf_op jit(solution)/shard_map/while/body/eval_jaxpr/qhd,khd->hqk/dot_general | solution.py:226
  395.7 5.7 copy-done
  401.4 6.7 fusion.159
  408.1 12.7 %fusion.156 = (f32[8]{0:T(128)S(1)}, bf16[8,1024,512]{1,2,0:T(8,128)(2,1)S(1)}) fusion(f32[8,512,1024]{2,1,0:T(8,128)} %copy-done, f32[8,1024]{1,0:T(8,128)} %get-tuple-element.906, bf16[1024,8,32]{0,2,1:T(8,128)(2,1)} %get-tuple-element.905, bf16[4,512,8,32]{1,3,2,0:T(8,128)(2,1)} %get-tuple-element.904, s32[]{:T(128)S(6)} %copy.150, ...), kind=kOutput, calls=%fused_computation.47.clone.1 | convolution fusion | flops 314572800 | bytes 26574916 | tf_op jit(solution)/shard_map/while/body/eval_jaxpr/qhd,khd->hqk/dot_general | solution.py:226
  442.5 128.2 %reduce-scatter.2.cloned.1.call-done = f32[64,512]{1,0:T(8,128)} async-done(((f32[2048,512]{1,0:T(8,128)}), f32[64,512]{1,0:T(8,128)}) %reduce-scatter.2.cloned.1.call-update) | async-done | bytes 131088 | tf_op jit(solution)/shard_map/reduce_scatter | solution.py:252
  577.5 37.4 %all-reduce.8 = (f32[6144]{0:T(1024)S(1)}, f32[1056]{0:T(1024)S(1)}) all-reduce(f32[6144]{0:T(1024)S(1)} %reshape.518, f32[1056]{0:T(1024)S(1)} %concatenate.15), channel_id=5, replica_groups=mesh['mem'=32] {'mem'}, use_global_device_ids=true, to_apply=%region_29.30.clone | all-reduce | flops 7200 | bytes 57600
  616.3 86.9 %all-reduce.14.cloned.1.call-done = (f32[196608]{0:T(1024)}, f32[65536]{0:T(1024)}) async-done(((f32[196608]{0:T(1024)}, f32[65536]{0:T(1024)}), (f32[196608]{0:T(1024)}, f32[65536]{0:T(1024)})) %all-reduce.14.cloned.1.call-update) | async-done | bytes 1048592
  708.6 39.4 %all-reduce.7 = (f32[32]{0:T(128)S(1)}, f32[]{:T(128)}, f32[]{:T(128)}) all-reduce(f32[32]{0:T(128)S(1)} %dynamic-update-slice.2, f32[]{:T(128)} %get-tuple-element.441, f32[]{:T(128)} %get-tuple-element.439), channel_id=1, replica_groups=mesh['mem'=32] {'mem'}, use_global_device_ids=true, to_apply=%add.2 | all-reduce | flops 34 | bytes 272
  (343 shorter events, 130.1 us)
Async XLA Ops:
  7.2 152.2 %copy-start.16 = (s32[1024]{0:T(1024)S(1)}, s32[1024]{0:T(1024)}, u32[]{:S(2)}) copy-start(s32[1024]{0:T(1024)} %param.29) | copy-start | bytes 12292
  7.2 143.3 %all-gather.2.cloned.1.call-start = ((), (), s32[]{:S(2)}) async-start(), calls=%async_computation.1 | async-start | bytes 2162688 | tf_op jit(solution)/shard_map/all_gather | solution.py:113
  52.6 106.8 %copy-start.33 = (f32[256]{0:T(256)}, f32[256]{0:T(256)S(1)}, u32[]{:S(2)}) copy-start(f32[256]{0:T(256)S(1)} %get-tuple-element.553) | copy-start | bytes 3076
  52.6 106.8 %copy-start.35 = (f32[256]{0:T(256)}, f32[256]{0:T(256)S(1)}, u32[]{:S(2)}) copy-start(f32[256]{0:T(256)S(1)} %get-tuple-element.554) | copy-start | bytes 3076
  52.6 106.8 %copy-start.37 = (f32[256]{0:T(256)}, f32[256]{0:T(256)S(1)}, u32[]{:S(2)}) copy-start(f32[256]{0:T(256)S(1)} %get-tuple-element.555) | copy-start | bytes 3076
  52.7 106.8 %copy-start.27 = (f32[8,32]{1,0:T(8,128)}, f32[8,32]{1,0:T(8,128)S(1)}, u32[]{:S(2)}) copy-start(f32[8,32]{1,0:T(8,128)S(1)} %add.202) | copy-start | bytes 3076
  52.8 106.7 %copy-start.28 = (f32[8,32]{1,0:T(8,128)}, f32[8,32]{1,0:T(8,128)S(1)}, u32[]{:S(2)}) copy-start(f32[8,32]{1,0:T(8,128)S(1)} %mul.534) | copy-start | bytes 3076
  97.8 472.9 %reduce-scatter.2.cloned.1.call-start = ((), (), s32[]{:S(2)}) async-start(), calls=%async_computation.2 | async-start | bytes 4325376 | tf_op jit(solution)/shard_map/reduce_scatter | solution.py:252
  278.5 151.6 %copy-start.25 = (f32[1024]{0:T(1024)S(1)}, f32[1024]{0:T(1024)}, u32[]{:S(2)}) copy-start(f32[1024]{0:T(1024)} %copy-done.24) | copy-start | bytes 12292
  278.5 152.7 %copy-start.4 = (bf16[1024,256]{0,1:T(8,128)(2,1)S(1)}, bf16[1024,256]{0,1:T(8,128)(2,1)}, u32[]{:S(2)}) copy-start(bf16[1024,256]{0,1:T(8,128)(2,1)} %copy-done.3) | copy-start | bytes 1572868
  278.5 157.9 %copy-start.7 = (bf16[256,768]{1,0:T(8,128)(2,1)S(1)}, bf16[256,768]{1,0:T(8,128)(2,1)}, u32[]{:S(2)}) copy-start(bf16[256,768]{1,0:T(8,128)(2,1)} %copy-done.6) | copy-start | bytes 1179652
  429.0 142.8 %copy-start.12 = (f32[64,256]{1,0:T(8,128)S(1)}, f32[64,256]{1,0:T(8,128)}, u32[]{:S(2)}) copy-start(f32[64,256]{1,0:T(8,128)} %copy-done.11) | copy-start | bytes 196612
  429.0 142.8 %copy-start.34 = (f32[256]{0:T(256)S(1)}, f32[256]{0:T(256)}, u32[]{:S(2)}) copy-start(f32[256]{0:T(256)} %copy-done.33) | copy-start | bytes 3076
  429.0 142.8 %copy-start.36 = (f32[256]{0:T(256)S(1)}, f32[256]{0:T(256)}, u32[]{:S(2)}) copy-start(f32[256]{0:T(256)} %copy-done.35) | copy-start | bytes 3076
  429.0 142.8 %copy-start.38 = (f32[256]{0:T(256)S(1)}, f32[256]{0:T(256)}, u32[]{:S(2)}) copy-start(f32[256]{0:T(256)} %copy-done.37) | copy-start | bytes 3076
  429.0 142.8 %copy-start.47 = (f32[64]{0:T(128)S(1)}, f32[64]{0:T(128)}, u32[]{:S(2)}) copy-start(f32[64]{0:T(128)} %copy-done.46) | copy-start | bytes 772
  429.1 142.8 %copy-start.51 = (f32[64]{0:T(128)S(1)}, f32[64]{0:T(128)}, u32[]{:S(2)}) copy-start(f32[64]{0:T(128)} %copy-done.50) | copy-start | bytes 772
  429.1 147.9 %copy-start.39 = (f32[64,8]{0,1:T(8,128)S(1)}, f32[64,8]{0,1:T(8,128)}, u32[]{:S(2)}) copy-start(f32[64,8]{0,1:T(8,128)} %param.32) | copy-start | bytes 6148
  429.1 148.4 %copy-start.54 = (f32[256]{0:T(256)S(1)}, f32[256]{0:T(256)}, u32[]{:S(2)}) copy-start(f32[256]{0:T(256)} %get-tuple-element.427) | copy-start | bytes 3076
  429.1 321.6 %copy-start.32 = (f32[6144]{0:T(1024)S(1)}, f32[6144]{0:T(1024)}, u32[]{:S(2)}) copy-start(f32[6144]{0:T(1024)} %param.36) | copy-start | bytes 73732
  429.1 321.6 %copy-start.41 = (f32[6144]{0:T(1024)S(1)}, f32[6144]{0:T(1024)}, u32[]{:S(2)}) copy-start(f32[6144]{0:T(1024)} %param.40) | copy-start | bytes 73732
  429.1 321.6 %copy-start.42 = (f32[6144]{0:T(1024)S(1)}, f32[6144]{0:T(1024)}, u32[]{:S(2)}) copy-start(f32[6144]{0:T(1024)} %param.44) | copy-start | bytes 73732
  429.1 323.0 %copy-start.40 = (f32[2048]{0:T(1024)S(1)}, f32[2048]{0:T(1024)}, u32[]{:S(2)}) copy-start(f32[2048]{0:T(1024)} %param.37) | copy-start | bytes 24580
  429.1 323.0 %copy-start.52 = (f32[2048]{0:T(1024)S(1)}, f32[2048]{0:T(1024)}, u32[]{:S(2)}) copy-start(f32[2048]{0:T(1024)} %param.41) | copy-start | bytes 24580
  429.2 323.0 %copy-start.53 = (f32[2048]{0:T(1024)S(1)}, f32[2048]{0:T(1024)}, u32[]{:S(2)}) copy-start(f32[2048]{0:T(1024)} %param.45) | copy-start | bytes 24580
  429.2 324.3 %copy-start.55 = (f32[192]{0:T(256)S(1)}, f32[192]{0:T(256)}, u32[]{:S(2)}) copy-start(f32[192]{0:T(256)} %param.38) | copy-start | bytes 2308
  429.2 324.3 %copy-start.56 = (f32[192]{0:T(256)S(1)}, f32[192]{0:T(256)}, u32[]{:S(2)}) copy-start(f32[192]{0:T(256)} %param.42) | copy-start | bytes 2308
  429.2 324.3 %copy-start.57 = (f32[192]{0:T(256)S(1)}, f32[192]{0:T(256)}, u32[]{:S(2)}) copy-start(f32[192]{0:T(256)} %param.46) | copy-start | bytes 2308
  429.2 325.0 %copy-start.58 = (f32[33]{0:T(128)S(1)}, f32[33]{0:T(128)}, u32[]{:S(2)}) copy-start(f32[33]{0:T(128)} %param.39) | copy-start | bytes 400
  429.2 325.0 %copy-start.59 = (f32[33]{0:T(128)S(1)}, f32[33]{0:T(128)}, u32[]{:S(2)}) copy-start(f32[33]{0:T(128)} %param.43) | copy-start | bytes 400
  429.2 324.9 %copy-start.60 = (f32[33]{0:T(128)S(1)}, f32[33]{0:T(128)}, u32[]{:S(2)}) copy-start(f32[33]{0:T(128)} %param.47) | copy-start | bytes 400
  429.3 273.9 %all-reduce.14.cloned.1.call-start = ((), (), s32[]{:S(2)}) async-start(), calls=%async_computation.3 | async-start | bytes 2097152
  (50 other events, 1171.2 us)
Sparse Core Ops, SparseCore 0:
  97.9 52.5 all-gather.1
  429.4 141.2 reduce-scatter.1
  576.9 126.2 all-reduce.13
